TPU v7x, 32 devices: a whole 2x2x4 slice. The times are simulated.
32 devices in a mesh: parts: 2 (over x), gx: 4 (over y, core), gy: 4 (over z).
Axes of the slice: x: 2, y: 2, z: 4, core: 2. Of those that a mesh axis runs over, the one named last changes fastest.
Arguments:
- forcing_right_side: float32 [32, 32, 1024], P(('parts', 'gx'), 'gy'), parts along dimension 0, may hold values from -18 to 18
- earlier_warmth: float32 [32, 32, 1024], P(('parts', 'gx'), 'gy'), parts along dimension 0, may hold values from 0 to 2
- matter_condition: int32 [32, 32, 1024], P(('parts', 'gx'), 'gy'), parts along dimension 0, may hold values from 0 to 2
- compressed_slot_number: int32 [32, 32, 1024], P(('parts', 'gx'), 'gy'), parts along dimension 0, may hold values from 0 to 127
- normal_draw_factor: float32 [32, 32, 1024], P(('parts', 'gx'), 'gy'), parts along dimension 0, may hold values from -6 to 6
Outputs:
- solution: float32 [32, 32, 1024], P(('parts', 'gx'), 'gy'), parts along dimension 0
- residual: float32 [32, 32, 1024], P(('parts', 'gx'), 'gy'), parts along dimension 0
There are 2 independent parts, one for each index of `parts`. A program takes and returns all parts, laid end to end along the dimension named above; each array names one. Nothing has to cross between parts.
Inputs may be any that keep to these rules, and one draw needn't show every extreme that they name: `matter_condition`: phase labels the cell as powder, solid or liquid. `compressed_slot_number`: each cell's row of the sketch.
All inputs are finite; a program needn't handle non-finite values.
Results may differ from a plain program's by a relative error of at most 0.0003.
Values sent between devices are 32-bit elements; how exact they have to be, the bound alone decides.
No kernel may reach another device: no remote copies, remote signals or barrier semaphores. Data moves between devices by JAX's collectives and lax.ppermute only.
A program may use at most 64 MiB of HBM per device.

v0:
```python
import jax
import jax.numpy as jnp
from jax import lax
from jax.experimental import pallas as pl
from jax.experimental.pallas import tpu as pltpu
from jax.sharding import PartitionSpec as P

SKETCH = 128
LOW = 32
HIGH = SKETCH // LOW
FIELDS = 3
LANES = 128
epsilon = 1e-06


def traits(warmth, phase):
    powder, solid = phase == 0, phase == 1
    offset = jnp.where(powder, 0.2, jnp.where(solid, 1.0, 0.6))
    return offset * (0.5 + warmth), jnp.where(powder, 1.0, jnp.where(solid, 2.0, 1.5))


def link(first, second):
    total = first + second
    return 2.0 * first * second / jnp.where(total > 0.0, total, 1.0)


def ahead(plane, axis):
    return pltpu.roll(plane, plane.shape[axis] - 1, axis)


def inner_links(cond):
    links = []
    for axis in (0, 1):
        index = lax.broadcasted_iota(jnp.int32, cond.shape, axis)
        links.append(
            jnp.where(index < cond.shape[axis] - 1, link(cond, ahead(cond, axis)), 0.0)
        )
    return links


def inner_flow(field, links):
    total = None
    for axis in (0, 1):
        flow = links[axis] * (field - ahead(field, axis))
        part = flow - pltpu.roll(flow, 1, axis)
        total = part if total is None else total + part
    return total


def apply_inside(images, c_wide, caps):
    results = []
    flow_low = link(c_wide[0], c_wide[1]) * (images[0] - images[1])
    for i in range(1, len(images) - 1):
        image = images[i]
        flow = link(c_wide[i], c_wide[i + 1]) * (image - images[i + 1])
        results.append(
            caps[i - 1] * image + inner_flow(image, inner_links(c_wide[i])) + (flow - flow_low)
        )
        flow_low = flow
    return results


def sketch_rows(fields, draws, slots, chosen, cells_ref):
    rows, depth = draws[0].shape
    for i, draw in enumerate(draws):
        coarse, fine = [], []
        for field in fields:
            weighted = draw * field[i]
            head = weighted.astype(jnp.bfloat16).astype(jnp.float32)
            coarse.append(head)
            fine.append(weighted - head)
        for f, part in enumerate(coarse + coarse[:1] + fine + fine[:1]):
            for t in range(depth // LANES):
                cells_ref[t, pl.ds(i * rows * 8 + f, rows, stride=8), :] = part[
                    :, t * LANES : (t + 1) * LANES
                ]
    low_index = lax.broadcasted_iota(jnp.int32, (LOW, depth), 0)
    low_index = low_index.astype(jnp.float32).astype(jnp.bfloat16)
    high_index = lax.broadcasted_iota(jnp.int32, (HIGH * 8, depth), 0) // 8
    high_index = high_index.astype(jnp.float32).astype(jnp.bfloat16)
    total = jnp.zeros((HIGH * 8, LOW), jnp.float32)
    for i, slot in enumerate(slots):
        low = (slot & (LOW - 1)).astype(jnp.float32)
        high = (slot >> (LOW.bit_length() - 1)).astype(jnp.float32)
        left, right = [], []
        for j in chosen:
            at = pl.ds((i * rows + j) * 8, 8)
            cells = [cells_ref[t, at, :] for t in range(depth // LANES)]
            cells = jnp.concatenate(cells, axis=1)
            cells = jnp.concatenate([cells] * HIGH, axis=0).astype(jnp.bfloat16)
            row_high = jnp.broadcast_to(high[j : j + 1], cells.shape).astype(jnp.bfloat16)
            row_low = jnp.broadcast_to(low[j : j + 1], (LOW, depth)).astype(jnp.bfloat16)
            left.append(jnp.where(row_high == high_index, cells, jnp.zeros_like(cells)))
            right.append(
                jnp.where(row_low == low_index, jnp.ones_like(row_low), jnp.zeros_like(row_low))
            )
        total = total + lax.dot_general(
            jnp.concatenate(left, axis=1),
            jnp.concatenate(right, axis=1),
            (((1,), (1,)), ((), ())),
            preferred_element_type=jnp.float32,
        )
    parts = jnp.concatenate([total[h * 8 : h * 8 + 8] for h in range(HIGH)], axis=1)
    return parts + pltpu.roll(parts, 4, 0)


def first_kernel(
    b_hbm, warmth_hbm, phase_hbm, b_ref, cond_ref, cap_ref, inner_ref, x_first_ref,
    x_second_ref, y_first_ref, y_second_ref, warmth_ref, phase_ref, arrived,
):
    copies = [
        pltpu.make_async_copy(source, target, arrived.at[k])
        for k, (source, target) in enumerate(
            ((b_hbm, b_ref), (warmth_hbm, warmth_ref), (phase_hbm, phase_ref))
        )
    ]
    for copy in copies:
        copy.start()
    for copy in copies:
        copy.wait()
    planes, rows = b_ref.shape[:2]
    images, conds = [], []
    for i in range(planes):
        cond, cap = traits(warmth_ref[i], phase_ref[i])
        cap_ref[i] = cap
        cond_ref[i] = cond
        field = b_ref[i]
        image = cap * field + inner_flow(field, inner_links(cond))
        if i:
            flow = link(conds[-1], cond) * (b_ref[i - 1] - field)
            images[-1] = images[-1] + flow
            image = image - flow
        conds.append(cond)
        images.append(image)
    for i in range(planes):
        inner_ref[i] = images[i]
    for k, field in enumerate((images, [b_ref[i] for i in range(planes)], conds)):
        x_first_ref[k], x_second_ref[k] = by_turn(field[0], field[-1], "gx")
        for i, plane in enumerate(field):
            at = slice(k * planes + i, k * planes + i + 1)
            y_first_ref[at], y_second_ref[at] = by_turn(plane[:1], plane[rows - 1 :], "gy")


def by_turn(one, other, axis):
    odd = lax.axis_index(axis) % 2 == 1
    return jnp.where(odd, one, other), jnp.where(odd, other, one)


def has_beside(axis):
    at = lax.axis_index(axis)
    return at > 0, at < lax.axis_size(axis) - 1


def second_kernel(
    b_ref, cond_ref, inner_ref, got_first_ref, got_second_ref, wide_ref, beside_ref, first_ref,
    second_ref,
):
    planes, rows = b_ref.shape[0], b_ref.shape[1]
    (image_low, image_high), (b_low, b_high), (c_low, c_high) = (
        by_turn(got_first_ref[k], got_second_ref[k], "gx") for k in range(3)
    )
    below, above = has_beside("gx")
    c_low, c_high = jnp.where(below, c_low, 0.0), jnp.where(above, c_high, 0.0)
    low_flow = link(c_low, cond_ref[0]) * (b_low - b_ref[0])
    high_flow = link(cond_ref[planes - 1], c_high) * (b_ref[planes - 1] - b_high)
    images = [image_low + low_flow] + [inner_ref[i] for i in range(planes)]
    images.append(image_high - high_flow)
    images[1] = images[1] - low_flow
    images[planes] = images[planes] + high_flow
    for i in range(planes + 2):
        wide_ref[i] = images[i]
    for k, plane in enumerate((b_low, b_high, c_low, c_high)):
        beside_ref[k] = plane
        at = slice(k, k + 1)
        first_ref[at], second_ref[at] = by_turn(plane[:1], plane[rows - 1 :], "gy")


def reached(rows):
    others = [j for j in range(rows) if 2 <= j < rows - 2]
    return [j for j in range(rows) if j not in others], others


def widened(ref, beside_ref, which):
    inner = [ref[i] for i in range(ref.shape[0])]
    return [beside_ref[which]] + inner + [beside_ref[which + 1]]


def inside_kernel(
    b_ref, cond_ref, cap_ref, slot_ref, draw_ref, wide_ref, beside_ref, sketch_ref,
    cells_ref,
):
    planes = range(b_ref.shape[0])
    images = [wide_ref[i] for i in range(wide_ref.shape[0])]
    c_wide = widened(cond_ref, beside_ref, 2)
    twice = apply_inside(images, c_wide, [cap_ref[i] for i in planes])
    sketch_ref[...] = sketch_rows(
        [[b_ref[i] for i in planes], images[1:-1], twice],
        [draw_ref[i] for i in planes],
        [slot_ref[i] for i in planes],
        reached(b_ref.shape[1])[1],
        cells_ref,
    )


def third_kernel(
    b_ref, cond_ref, cap_ref, slot_ref, draw_ref, wide_ref, beside_ref, got_first_ref,
    got_second_ref, corner_first_ref, corner_second_ref, inside_ref, image_ref, twice_ref, sketch_ref, cells_ref,
):
    planes, rows, depth = b_ref.shape
    index = lax.broadcasted_iota(jnp.int32, (rows, depth), 0)
    b_wide = widened(b_ref, beside_ref, 0)
    c_wide = widened(cond_ref, beside_ref, 2)
    lines = by_turn(got_first_ref[...], got_second_ref[...], "gy")
    corners = by_turn(corner_first_ref[...], corner_second_ref[...], "gy")
    images = [wide_ref[i] for i in range(planes + 2)]
    beside = []
    for j, here, line, corner in zip((0, rows - 1), has_beside("gy"), lines, corners):
        parts = [[line[k * planes + i :][:1] for i in range(planes)] for k in range(3)]
        beyond, b_line, c_line = parts
        b_line = [corner[0:1]] + b_line + [corner[1:2]]
        c_line = [corner[2:3]] + c_line + [corner[3:4]]
        c_line = [jnp.where(here, c, 0.0) for c in c_line]
        beyond[0] = beyond[0] + link(c_line[0], c_line[1]) * (b_line[1] - b_line[0])
        beyond[-1] = beyond[-1] + link(c_line[-2], c_line[-1]) * (b_line[-2] - b_line[-1])
        for i in range(planes + 2):
            conductance = link(c_wide[i], jnp.broadcast_to(c_line[i], (rows, depth)))
            conductance = jnp.where(index == j, conductance, 0.0)
            flow = conductance * (b_wide[i] - b_line[i])
            images[i] = images[i] + flow
            if 0 < i <= planes:
                beside.append((i, conductance, beyond[i - 1] - flow))
    twice = apply_inside(images, c_wide, [cap_ref[i] for i in range(planes)])
    for i, conductance, value in beside:
        twice[i - 1] = twice[i - 1] + conductance * (images[i] - value)
    for i in range(planes):
        image_ref[i] = images[i + 1]
        twice_ref[i] = twice[i]
    sketch = inside_ref[...] + sketch_rows(
        [b_wide[1:-1], images[1:-1], twice],
        [draw_ref[i] for i in range(planes)],
        [slot_ref[i] for i in range(planes)],
        reached(rows)[0],
        cells_ref,
    )
    sketch_ref[...] = sketch[: FIELDS + 1]


def last_kernel(sketch_ref, b_ref, image_ref, twice_ref, solution_ref, residual_ref):
    sketches = jnp.sum(sketch_ref[...], axis=0)

    def inner(first, second):
        return jnp.sum(first * second, axis=1, keepdims=True)

    s0, s1, s2 = (sketches[i : i + 1] for i in range(FIELDS))
    beta = jnp.sqrt(inner(s0, s0) + epsilon)
    q0 = s0 / beta
    p0 = s1 / beta
    h00 = inner(q0, p0)
    t0 = p0 - h00 * q0
    n0 = jnp.sqrt(inner(t0, t0) + epsilon)
    q1 = t0 / n0
    p1 = (s2 / beta - h00 * p0) / n0
    h01 = inner(q0, p1)
    h11 = inner(q1, p1)
    t1 = p1 - h01 * q0 - h11 * q1
    n1 = jnp.sqrt(inner(t1, t1) + epsilon)
    l00 = jnp.sqrt(h00 * h00 + n0 * n0)
    l10 = (h00 * h01 + n0 * h11) / l00
    l11 = jnp.sqrt(h01 * h01 + h11 * h11 + n1 * n1 - l10 * l10)
    z0 = beta * h00 / l00
    z1 = (beta * h01 - l10 * z0) / l11
    y1 = z1 / l11
    y0 = (z0 - l10 * y1) / l00
    c1 = y1 / (beta * n0)
    c0 = y0 / beta - h00 * c1
    for i in range(b_ref.shape[0]):
        b, image = b_ref[i], image_ref[i]
        solution_ref[i] = c0 * b + c1 * image
        residual_ref[i] = b - c0 * image - c1 * twice_ref[i]


def call(kernel, shapes, *operands, scratch=(), inputs=pltpu.VMEM, flops=0):
    return pl.pallas_call(
        kernel,
        out_shape=[jax.ShapeDtypeStruct(shape, jnp.float32) for shape in shapes],
        in_specs=[pl.BlockSpec(memory_space=inputs)] * len(operands),
        out_specs=[pl.BlockSpec(memory_space=pltpu.VMEM)] * len(shapes),
        scratch_shapes=scratch,
        compiler_params=pltpu.CompilerParams(vmem_limit_bytes=48 * 1024 * 1024),
        cost_estimate=pl.CostEstimate(flops=flops, bytes_accessed=0, transcendentals=0),
    )(*operands)


def swap(first, second, axis):
    across = "gy" if axis == "gx" else "gx"
    count, lines = lax.axis_size(axis), lax.axis_size(across)

    def number(place, line):
        at = (place, line) if axis == "gx" else (line, place)
        return at[0] * lax.axis_size("gy") + at[1]

    turns = ([], [])
    for line in range(lines):
        for i in range(count):
            turns[0].append((number(i, line), number(i ^ 1, line)))
            beyond = i + 1 if i % 2 else i - 1
            if 0 <= beyond < count:
                turns[1].append((number(i, line), number(beyond, line)))
            else:
                turns[1].append((number(i, line), number(i, line ^ 1)))
    return [lax.ppermute(x, ("gx", "gy"), turn) for x, turn in zip((first, second), turns)]


def everyones(sketch):
    count = lax.axis_size("gx") * lax.axis_size("gy")
    copies = jnp.broadcast_to(sketch[None], (count,) + sketch.shape)
    return lax.all_to_all(copies, ("gx", "gy"), 0, 0)


def body(b, warmth, phase, slots, draw):
    planes, rows, depth = b.shape
    block, plane, wide = b.shape, (3, rows, depth), (planes + 2, rows, depth)
    line, corner, table = (3 * planes, depth), (4, depth), (8, SKETCH)
    cells = pltpu.VMEM((depth // LANES, planes * rows * 8, LANES), jnp.float32)
    work = b.size * SKETCH * 6
    b, cond, cap, inner, x_first, x_second, y_first, y_second = call(
        first_kernel,
        [block, block, block, block, plane, plane, line, line],
        *(pltpu.with_memory_space_constraint(x, pltpu.HBM) for x in (b, warmth, phase)),
        scratch=[
            pltpu.VMEM(block, warmth.dtype),
            pltpu.VMEM(block, phase.dtype),
            pltpu.SemaphoreType.DMA((3,)),
        ],
        inputs=pltpu.HBM,
    )
    got_x = swap(x_first, x_second, "gx")
    got_y = swap(y_first, y_second, "gy")
    image_wide, beside, first, second = call(
        second_kernel, [wide, (4, rows, depth), corner, corner], b, cond, inner, *got_x
    )
    got_corners = swap(first, second, "gy")
    (inside,) = call(
        inside_kernel,
        [table],
        b, cond, cap, slots, draw, image_wide, beside,
        scratch=[cells],
        flops=work,
    )
    image, twice, sketch = call(
        third_kernel,
        [block, block, (FIELDS + 1, SKETCH)],
        b, cond, cap, slots, draw, image_wide, beside, *got_y, *got_corners, inside,
        scratch=[cells],
        flops=work,
    )
    return tuple(call(last_kernel, [block, block], everyones(sketch), b, image, twice))


def solution(mesh):
    spec = P(("parts", "gx"), "gy", None)
    return jax.shard_map(
        body, mesh=mesh, in_specs=(spec,) * 5, out_specs=(spec,) * 2, check_vma=False
    )
```

profile of v0, /device:TPU:0, one launch (start us, length us, event | category | flops | bytes accessed | tf_op | source)
XLA Modules:
  0.0 26.7 jit_solution(1915678523123622139)
XLA Ops:
  0.6 1.4 %shard_map.68 = (f32[4,8,1024]{2,1,0:T(8,128)S(1)}, f32[4,8,1024]{2,1,0:T(8,128)S(1)}, f32[4,8,1024]{2,1,0:T(8,128)S(1)}, f32[4,8,1024]{2,1,0:T(8,128)S(1)}, f32...) custom-call(f32[4,8,1024]{2,1,0:T(8,128)} %b_hbm.1, ...), custom_call_target="tpu_custom_call" | custom-call | tf_op jit(solution)/shard_map/pallas_call | solution.py:283
  2.0 0.5 %collective-permute-start = (f32[3,8,1024]{2,1,0:T(8,128)S(1)}, f32[3,8,1024]{2,1,0:T(8,128)S(1)}, u32[]{:S(2)}, u32[]{:S(2)}) collective-permute-start(f32[3,8,1024]{2,1,0:T(8,128)S(1)} %get-tuple-element.21), channel_id=1, source_target_pairs={{0,4},{4,0},{8,12},{12,8},{1,5},{5,1},{9,13},{13,9},{2,6},{6,2},{1... | collective-permute-start | bytes 294920 | tf_op jit(solution)/shard_map/ppermute | solution.py:311
  2.5 2.6 %collective-permute-start.1 = (f32[3,8,1024]{2,1,0:T(8,128)S(1)}, f32[3,8,1024]{2,1,0:T(8,128)S(1)}, u32[]{:S(2)}, u32[]{:S(2)}) collective-permute-start(f32[3,8,1024]{2,1,0:T(8,128)S(1)} %get-tuple-element.22), channel_id=1, source_target_pairs={{0,1},{4,8},{8,4},{12,13},{1,0},{5,9},{9,5},{13,12},{2,3},{6,10},{... | collective-permute-start | bytes 294920 | tf_op jit(solution)/shard_map/ppermute | solution.py:311
  5.2 0.1 collective-permute-start.2
  5.3 1.3 %collective-permute-start.3 = (f32[12,1024]{1,0:T(8,128)S(1)}, f32[12,1024]{1,0:T(8,128)S(1)}, u32[]{:S(2)}, u32[]{:S(2)}) collective-permute-start(f32[12,1024]{1,0:T(8,128)S(1)} %get-tuple-element.26), channel_id=1, source_target_pairs={{0,4},{1,2},{2,1},{3,7},{4,0},{5,6},{6,5},{7,3},{8,12},{9,10},{10,... | collective-permute-start | bytes 147464 | tf_op jit(solution)/shard_map/ppermute | solution.py:311
  6.5 0.0 collective-permute-done.got_first_ref
  6.5 1.2 %collective-permute-done.1.got_second_ref = f32[3,8,1024]{2,1,0:T(8,128)S(1)} collective-permute-done((f32[3,8,1024]{2,1,0:T(8,128)S(1)}, f32[3,8,1024]{2,1,0:T(8,128)S(1)}, u32[]{:S(2)}, u32[]{:S(2)}) %collective-permute-start.1) | collective-permute-done | bytes 98336 | tf_op jit(solution)/shard_map/ppermute | solution.py:311
  7.8 0.0 copy-start
  7.8 0.0 copy-start.1
  7.8 0.1 shard_map.69
  7.9 2.5 %collective-permute-start.4 = (f32[4,1024]{1,0:T(4,128)S(1)}, f32[4,1024]{1,0:T(4,128)S(1)}, u32[]{:S(2)}, u32[]{:S(2)}) collective-permute-start(f32[4,1024]{1,0:T(4,128)S(1)} %get-tuple-element.27), channel_id=1, source_target_pairs={{0,1},{1,0},{2,3},{3,2},{4,5},{5,4},{6,7},{7,6},{8,9},{9,8},{10,11... | collective-permute-start | bytes 49160 | tf_op jit(solution)/shard_map/ppermute | solution.py:311
  10.4 0.0 collective-permute-start.5
  10.4 0.0 copy-done
  10.4 0.0 copy-done.1
  10.4 0.8 %shard_map.70.inside_ref = f32[8,128]{1,0:T(8,128)S(1)} custom-call(f32[4,8,1024]{2,1,0:T(8,128)S(1)} %get-tuple-element.17.b_ref, f32[4,8,1024]{2,1,0:T(8,128)S(1)} %get-tuple-element.18.cond_ref, f32[4,8,1024]{2,1,0:T(8,128)S(1)} %get-tuple-element.19.cap_ref, s32[4,8,1024]{2,1,0:T(8,128)S(1)} %copy-done, f32[4,8,1024]{2,1,0:T(8,128)S(1)} %copy-done.1, ...), custom_call_target="tpu_custom_call" | custom-call | flops 25165824 | tf_op jit(solution)/shard_map/pallas_call | solution.py:283
  11.2 0.0 collective-permute-done.2.got_first_ref
  11.2 0.0 collective-permute-done.3.got_second_ref
  11.3 0.8 %collective-permute-done.4.corner_first_ref = f32[4,1024]{1,0:T(4,128)S(1)} collective-permute-done((f32[4,1024]{1,0:T(4,128)S(1)}, f32[4,1024]{1,0:T(4,128)S(1)}, u32[]{:S(2)}, u32[]{:S(2)}) %collective-permute-start.4) | collective-permute-done | bytes 16416 | tf_op jit(solution)/shard_map/ppermute | solution.py:311
  12.1 0.0 collective-permute-done.5.corner_second_ref
  12.1 1.1 %shard_map.71 = (f32[4,8,1024]{2,1,0:T(8,128)S(1)}, f32[4,8,1024]{2,1,0:T(8,128)S(1)}, f32[4,128]{1,0:T(4,128)S(1)}) custom-call(f32[4,8,1024]{2,1,0:T(8,128)S(1)} %get-tuple-element.17.b_ref, f32[4,8,1024]{2,1,0:T(8,128)S(1)} %get-tuple-element.18.cond_ref, f32[4,8,1024]{2,1,0:T(8,128)S(1)} %get-tuple-element.19.cap_ref, s32[4,8,1024]{2,1,0:T(8,128)S(1)} %copy-done, ...), custom_call_target="tpu_custom_call" | custom-call | flops 25165824 | tf_op jit(solution)/shard_map/pallas_call | solution.py:283
  13.2 12.3 %all_to_all.5.sketch_ref = f32[16,4,128]{2,1,0:T(4,128)S(1)} all-to-all(f32[16,4,128]{2,1,0:T(4,128)S(1)} %broadcast_in_dim.2), channel_id=1, replica_groups=mesh['parts'=2,'gx'=4,'gy'=4] {'gx','gy'}, dimensions={0} | all-to-all | bytes 65536 | tf_op jit(solution)/shard_map/all_to_all | solution.py:317
  25.5 1.2 %shard_map.72 = (f32[4,8,1024]{2,1,0:T(8,128)}, f32[4,8,1024]{2,1,0:T(8,128)}) custom-call(f32[16,4,128]{2,1,0:T(4,128)S(1)} %all_to_all.5.sketch_ref, f32[4,8,1024]{2,1,0:T(8,128)S(1)} %get-tuple-element.17.b_ref, f32[4,8,1024]{2,1,0:T(8,128)S(1)} %get-tuple-element.30.image_ref, f32[4,8,1024]{2,1,0:T(8,128)S(1)} %get-tuple-element.31.twice_ref), custom_call_target="tpu_custom_call" | custom-call | tf_op jit(solution)/shard_map/pallas_call | solution.py:283
  (1 shorter events, 0.0 us)
Async XLA Ops:
  2.0 4.5 %collective-permute-start = (f32[3,8,1024]{2,1,0:T(8,128)S(1)}, f32[3,8,1024]{2,1,0:T(8,128)S(1)}, u32[]{:S(2)}, u32[]{:S(2)}) collective-permute-start(f32[3,8,1024]{2,1,0:T(8,128)S(1)} %get-tuple-element.21), channel_id=1, source_target_pairs={{0,4},{4,0},{8,12},{12,8},{1,5},{5,1},{9,13},{13,9},{2,6},{6,2},{1... | collective-permute-start | bytes 294920 | tf_op jit(solution)/shard_map/ppermute | solution.py:311
  2.5 5.2 %collective-permute-start.1 = (f32[3,8,1024]{2,1,0:T(8,128)S(1)}, f32[3,8,1024]{2,1,0:T(8,128)S(1)}, u32[]{:S(2)}, u32[]{:S(2)}) collective-permute-start(f32[3,8,1024]{2,1,0:T(8,128)S(1)} %get-tuple-element.22), channel_id=1, source_target_pairs={{0,1},{4,8},{8,4},{12,13},{1,0},{5,9},{9,5},{13,12},{2,3},{6,10},{... | collective-permute-start | bytes 294920 | tf_op jit(solution)/shard_map/ppermute | solution.py:311
  5.2 6.1 %collective-permute-start.2 = (f32[12,1024]{1,0:T(8,128)S(1)}, f32[12,1024]{1,0:T(8,128)S(1)}, u32[]{:S(2)}, u32[]{:S(2)}) collective-permute-start(f32[12,1024]{1,0:T(8,128)S(1)} %get-tuple-element.25), channel_id=1, source_target_pairs={{0,1},{1,0},{2,3},{3,2},{4,5},{5,4},{6,7},{7,6},{8,9},{9,8},{10,11... | collective-permute-start | bytes 147464 | tf_op jit(solution)/shard_map/ppermute | solution.py:311
  5.3 6.0 %collective-permute-start.3 = (f32[12,1024]{1,0:T(8,128)S(1)}, f32[12,1024]{1,0:T(8,128)S(1)}, u32[]{:S(2)}, u32[]{:S(2)}) collective-permute-start(f32[12,1024]{1,0:T(8,128)S(1)} %get-tuple-element.26), channel_id=1, source_target_pairs={{0,4},{1,2},{2,1},{3,7},{4,0},{5,6},{6,5},{7,3},{8,12},{9,10},{10,... | collective-permute-start | bytes 147464 | tf_op jit(solution)/shard_map/ppermute | solution.py:311
  7.8 2.6 %copy-start = (s32[4,8,1024]{2,1,0:T(8,128)S(1)}, s32[4,8,1024]{2,1,0:T(8,128)}, u32[]{:S(2)}) copy-start(s32[4,8,1024]{2,1,0:T(8,128)} %slot_ref.3) | copy-start | bytes 393220
  7.8 2.6 %copy-start.1 = (f32[4,8,1024]{2,1,0:T(8,128)S(1)}, f32[4,8,1024]{2,1,0:T(8,128)}, u32[]{:S(2)}) copy-start(f32[4,8,1024]{2,1,0:T(8,128)} %draw_ref.3) | copy-start | bytes 393220
  7.9 4.2 %collective-permute-start.4 = (f32[4,1024]{1,0:T(4,128)S(1)}, f32[4,1024]{1,0:T(4,128)S(1)}, u32[]{:S(2)}, u32[]{:S(2)}) collective-permute-start(f32[4,1024]{1,0:T(4,128)S(1)} %get-tuple-element.27), channel_id=1, source_target_pairs={{0,1},{1,0},{2,3},{3,2},{4,5},{5,4},{6,7},{7,6},{8,9},{9,8},{10,11... | collective-permute-start | bytes 49160 | tf_op jit(solution)/shard_map/ppermute | solution.py:311
  10.4 1.7 %collective-permute-start.5 = (f32[4,1024]{1,0:T(4,128)S(1)}, f32[4,1024]{1,0:T(4,128)S(1)}, u32[]{:S(2)}, u32[]{:S(2)}) collective-permute-start(f32[4,1024]{1,0:T(4,128)S(1)} %get-tuple-element.28), channel_id=1, source_target_pairs={{0,4},{1,2},{2,1},{3,7},{4,0},{5,6},{6,5},{7,3},{8,12},{9,10},{10,... | collective-permute-start | bytes 49160 | tf_op jit(solution)/shard_map/ppermute | solution.py:311
where the time goes:
time: 26.9 us; the launch traced here: 26.7 us
  blocking collectives  12.3 us (46%)
  starting transfers between devices  7.04 us (26%)
  Pallas kernels  4.61 us (17%)
  waiting for transfers between devices  2.1 us (8%)
  between operations  0.67 us (2%)
    all_to_all x1, blocking collectives, everyones(): return lax.all_to_all(copies, ('gx', 'gy'), 0, 0)  12.3 us
    ppermute x6, starting transfers between devices, swap(): lax.ppermute(x, ('gx', 'gy'), turn)  7.04 us
    pallas_call x5, Pallas kernels, call(): pl.pallas_call(kernel, out_shape=[jax.ShapeDtypeStruct(shape, jnp.float32...  4.61 us
    ppermute x6, waiting for transfers between devices, swap(): lax.ppermute(x, ('gx', 'gy'), turn)  2.1 us
  transfers between devices with their start and end apart: 6, of which 2 were waited for; matrix products, arithmetic and copies ran while one was open for 0% of the time, Pallas kernels for 3%

commit v1 on v0

v1 whole, which is shorter than its diff:
```python
import jax
import jax.numpy as jnp
from jax import lax
from jax.experimental import pallas as pl
from jax.experimental.pallas import tpu as pltpu
from jax.sharding import PartitionSpec as P

SKETCH = 128
LOW = 32
HIGH = SKETCH // LOW
FIELDS = 3
LANES = 128
epsilon = 1e-06


def traits(warmth, phase):
    powder, solid = phase == 0, phase == 1
    offset = jnp.where(powder, 0.2, jnp.where(solid, 1.0, 0.6))
    return offset * (0.5 + warmth), jnp.where(powder, 1.0, jnp.where(solid, 2.0, 1.5))


def link(first, second):
    total = first + second
    return 2.0 * first * second / jnp.where(total > 0.0, total, 1.0)


def ahead(plane, axis):
    return pltpu.roll(plane, plane.shape[axis] - 1, axis)


def inner_links(cond):
    links = []
    for axis in (0, 1):
        index = lax.broadcasted_iota(jnp.int32, cond.shape, axis)
        links.append(
            jnp.where(index < cond.shape[axis] - 1, link(cond, ahead(cond, axis)), 0.0)
        )
    return links


def inner_flow(field, links):
    total = None
    for axis in (0, 1):
        flow = links[axis] * (field - ahead(field, axis))
        part = flow - pltpu.roll(flow, 1, axis)
        total = part if total is None else total + part
    return total


def apply_inside(images, c_wide, caps):
    results = []
    flow_low = link(c_wide[0], c_wide[1]) * (images[0] - images[1])
    for i in range(1, len(images) - 1):
        image = images[i]
        flow = link(c_wide[i], c_wide[i + 1]) * (image - images[i + 1])
        results.append(
            caps[i - 1] * image + inner_flow(image, inner_links(c_wide[i])) + (flow - flow_low)
        )
        flow_low = flow
    return results


def sketch_rows(planes, cells_ref):
    depth = cells_ref.shape[0] * LANES
    low_index = lax.broadcasted_iota(jnp.int32, (LOW, depth), 0)
    low_index = low_index.astype(jnp.float32).astype(jnp.bfloat16)
    high_index = lax.broadcasted_iota(jnp.int32, (HIGH * 8, depth), 0) // 8
    high_index = high_index.astype(jnp.float32).astype(jnp.bfloat16)
    total = jnp.zeros((HIGH * 8, LOW), jnp.float32)
    start = 0
    for fields, draw, slot, chosen in planes:
        rows = draw.shape[0]
        coarse, fine = [], []
        for field in fields:
            weighted = draw * field
            head = weighted.astype(jnp.bfloat16).astype(jnp.float32)
            coarse.append(head)
            fine.append(weighted - head)
        for f, part in enumerate(coarse + coarse[:1] + fine + fine[:1]):
            for t in range(depth // LANES):
                cells_ref[t, pl.ds(start + f, rows, stride=8), :] = part[
                    :, t * LANES : (t + 1) * LANES
                ]
        high = jnp.floor(slot * (1.0 / LOW))
        low = slot - LOW * high
        left, right = [], []
        for j in chosen:
            at = pl.ds(start + j * 8, 8)
            cells = [cells_ref[t, at, :] for t in range(depth // LANES)]
            cells = jnp.concatenate(cells, axis=1)
            cells = jnp.concatenate([cells] * HIGH, axis=0).astype(jnp.bfloat16)
            row_high = jnp.broadcast_to(high[j : j + 1], cells.shape).astype(jnp.bfloat16)
            row_low = jnp.broadcast_to(low[j : j + 1], (LOW, depth)).astype(jnp.bfloat16)
            left.append(jnp.where(row_high == high_index, cells, jnp.zeros_like(cells)))
            right.append(
                jnp.where(row_low == low_index, jnp.ones_like(row_low), jnp.zeros_like(row_low))
            )
        total = total + lax.dot_general(
            jnp.concatenate(left, axis=1),
            jnp.concatenate(right, axis=1),
            (((1,), (1,)), ((), ())),
            preferred_element_type=jnp.float32,
        )
        start += rows * 8
    parts = jnp.concatenate([total[h * 8 : h * 8 + 8] for h in range(HIGH)], axis=1)
    return parts + pltpu.roll(parts, 4, 0)


def first_kernel(
    b_hbm, warmth_hbm, phase_hbm, draw_hbm, slot_hbm, b_ref, cond_ref, cap_ref, inner_ref,
    draw_ref, slot_ref, x_first_ref, x_second_ref, y_first_ref, y_second_ref, warmth_ref,
    phase_ref, number_ref, arrived,
):
    copies = [
        pltpu.make_async_copy(source, target, arrived.at[k])
        for k, (source, target) in enumerate(
            (
                (b_hbm, b_ref),
                (warmth_hbm, warmth_ref),
                (phase_hbm, phase_ref),
                (draw_hbm, draw_ref),
                (slot_hbm, number_ref),
            )
        )
    ]
    for copy in copies:
        copy.start()
    for copy in copies[:3]:
        copy.wait()
    planes, rows = b_ref.shape[:2]
    images, conds = [], []
    for i in range(planes):
        cond, cap = traits(warmth_ref[i], phase_ref[i])
        cap_ref[i] = cap
        cond_ref[i] = cond
        field = b_ref[i]
        image = cap * field + inner_flow(field, inner_links(cond))
        if i:
            flow = link(conds[-1], cond) * (b_ref[i - 1] - field)
            images[-1] = images[-1] + flow
            image = image - flow
        conds.append(cond)
        images.append(image)
    for i in range(planes):
        inner_ref[i] = images[i]
    for k, field in enumerate((images, [b_ref[i] for i in range(planes)], conds)):
        at = slice(k * rows, (k + 1) * rows)
        x_first_ref[at], x_second_ref[at] = by_turn(field[0], field[-1], "gx")
        for i, plane in enumerate(field):
            at = slice(k * planes + i, k * planes + i + 1)
            y_first_ref[at], y_second_ref[at] = by_turn(plane[:1], plane[rows - 1 :], "gy")
    for copy in copies[3:]:
        copy.wait()
    for i in range(planes):
        slot_ref[i] = number_ref[i].astype(jnp.float32)
    for k, ref in enumerate((draw_ref, slot_ref)):
        ends = [ref[0], ref[planes - 1]]
        for e, j in enumerate((0, rows - 1)):
            at = slice(3 * rows + 2 * k + e, 3 * rows + 2 * k + e + 1)
            lines = [plane[j : j + 1] for plane in ends]
            x_first_ref[at], x_second_ref[at] = by_turn(*lines, "gx")
        for e, plane in enumerate(ends):
            at = slice(3 * planes + 2 * k + e, 3 * planes + 2 * k + e + 1)
            lines = [plane[:1], plane[rows - 1 :]]
            y_first_ref[at], y_second_ref[at] = by_turn(*lines, "gy")


def by_turn(one, other, axis):
    odd = lax.axis_index(axis) % 2 == 1
    return jnp.where(odd, one, other), jnp.where(odd, other, one)


def has_beside(axis):
    at = lax.axis_index(axis)
    return at > 0, at < lax.axis_size(axis) - 1


def reached(rows):
    others = [j for j in range(rows) if 2 <= j < rows - 2]
    return [j for j in range(rows) if j not in others], others


def widened(ref, beside_ref, which):
    inner = [ref[i] for i in range(ref.shape[0])]
    return [beside_ref[which]] + inner + [beside_ref[which + 1]]


def inside_kernel(
    b_ref, cond_ref, cap_ref, inner_ref, draw_ref, slot_ref, got_first_ref, got_second_ref,
    wide_ref, beside_ref, sketch_ref, cells_ref,
):
    planes, rows = b_ref.shape[:2]
    (image_low, image_high), (b_low, b_high), (c_low, c_high) = (
        by_turn(*(ref[k * rows : (k + 1) * rows] for ref in (got_first_ref, got_second_ref)), "gx")
        for k in range(3)
    )
    below, above = has_beside("gx")
    c_low, c_high = jnp.where(below, c_low, 0.0), jnp.where(above, c_high, 0.0)
    for k, plane in enumerate((b_low, b_high, c_low, c_high)):
        beside_ref[k] = plane
    c_wide = [c_low] + [cond_ref[i] for i in range(planes)] + [c_high]
    low_flow = link(c_low, c_wide[1]) * (b_low - b_ref[0])
    high_flow = link(c_wide[-2], c_high) * (b_ref[planes - 1] - b_high)
    images = [image_low + low_flow] + [inner_ref[i] for i in range(planes)]
    images.append(image_high - high_flow)
    images[1] = images[1] - low_flow
    images[-2] = images[-2] + high_flow
    for i, image in enumerate(images):
        wide_ref[i] = image
    twice = apply_inside(images, c_wide, [cap_ref[i] for i in range(planes)])
    chosen = reached(rows)[1]
    sketch_ref[...] = sketch_rows(
        [
            ((b_ref[i], images[i + 1], twice[i]), draw_ref[i], slot_ref[i], chosen)
            for i in range(planes)
        ],
        cells_ref,
    )


def third_kernel(
    b_ref, cond_ref, cap_ref, draw_ref, slot_ref, wide_ref, beside_ref, x_first_ref,
    x_second_ref, y_first_ref, y_second_ref, inside_ref, image_ref, twice_ref, sketch_ref,
    corner_first_ref, corner_second_ref, ends_ref, cells_ref, extra_ref,
):
    planes, rows, depth = b_ref.shape
    index = lax.broadcasted_iota(jnp.int32, (rows, depth), 0)
    b_wide = widened(b_ref, beside_ref, 0)
    c_wide = widened(cond_ref, beside_ref, 2)
    images = [wide_ref[i] for i in range(planes + 2)]
    x_ends = []
    for inner, outer in ((1, 0), (planes, planes + 1)):
        conductance = link(c_wide[inner], c_wide[outer])
        x_ends.append((inner, outer, conductance, conductance * (b_wide[inner] - b_wide[outer])))
    x_tails = by_turn(x_first_ref[3 * rows :], x_second_ref[3 * rows :], "gx")
    y_lines = by_turn(y_first_ref[...], y_second_ref[...], "gy")
    beside = []
    for side, (j, here, line) in enumerate(zip((0, rows - 1), has_beside("gy"), y_lines)):
        row = slice(j, j + 1)
        parts = [[line[k * planes + i :][:1] for i in range(planes)] for k in range(3)]
        beyond, b_line, c_line = parts
        c_line = [jnp.where(here, c, 0.0) for c in c_line]
        flows = []
        for i in range(planes):
            conductance = link(c_wide[i + 1], jnp.broadcast_to(c_line[i], (rows, depth)))
            conductance = jnp.where(index == j, conductance, 0.0)
            flow = conductance * (b_wide[i + 1] - b_line[i])
            images[i + 1] = images[i + 1] + flow
            beside.append((i, conductance, beyond[i] - flow))
            flows.append((conductance, flow))
        for end, (inner, outer, x_link, x_flow) in enumerate(x_ends):
            y_link, y_flow = flows[inner - 1]
            at = 4 * side + 2 * end
            tail = x_tails[end]
            values = (-x_link * y_flow)[row], tail[side : side + 1], tail[2 + side : 3 + side]
            for k, value in enumerate(values):
                extra_ref[k, at : at + 1] = value
            tail = line[3 * planes :]
            values = (-y_link * x_flow)[row], tail[end : end + 1], tail[2 + end : 3 + end]
            for k, value in enumerate(values):
                extra_ref[k, at + 1 : at + 2] = value
            at = 6 * (2 * side + end)
            values = x_link, b_wide[outer], c_wide[outer], y_link
            for k, value in enumerate(values):
                ends_ref[at + k : at + k + 1] = value[row]
            ends_ref[at + 4 : at + 5] = b_line[inner - 1]
            ends_ref[at + 5 : at + 6] = c_line[inner - 1]
    twice = apply_inside(images, c_wide, [cap_ref[i] for i in range(planes)])
    for i, conductance, value in beside:
        twice[i] = twice[i] + conductance * (images[i + 1] - value)
    for i in range(planes):
        image_ref[i] = images[i + 1]
        twice_ref[i] = twice[i]
    chosen = reached(rows)[0]
    cells = [
        ((b_wide[i + 1], images[i + 1], twice[i]), draw_ref[i], slot_ref[i], chosen)
        for i in range(planes)
    ]
    extra, nothing = [extra_ref[k] for k in range(3)], jnp.zeros((8, depth), jnp.float32)
    cells.append(((nothing, nothing, extra[0]), extra[1], extra[2], range(8)))
    sketch = inside_ref[...] + sketch_rows(cells, cells_ref)
    sketch_ref[...] = sketch[: FIELDS + 1]
    for k, plane in enumerate((b_wide[0], b_wide[-1], c_wide[0], c_wide[-1])):
        at = slice(k, k + 1)
        corner_first_ref[at], corner_second_ref[at] = by_turn(
            plane[:1], plane[rows - 1 :], "gy"
        )


def last_kernel(
    sketch_ref, b_ref, image_ref, twice_ref, ends_ref, corner_first_ref, corner_second_ref,
    solution_ref, residual_ref,
):
    sketches = jnp.sum(sketch_ref[...], axis=0)

    def inner(first, second):
        return jnp.sum(first * second, axis=1, keepdims=True)

    s0, s1, s2 = (sketches[i : i + 1] for i in range(FIELDS))
    beta = jnp.sqrt(inner(s0, s0) + epsilon)
    q0 = s0 / beta
    p0 = s1 / beta
    h00 = inner(q0, p0)
    t0 = p0 - h00 * q0
    n0 = jnp.sqrt(inner(t0, t0) + epsilon)
    q1 = t0 / n0
    p1 = (s2 / beta - h00 * p0) / n0
    h01 = inner(q0, p1)
    h11 = inner(q1, p1)
    t1 = p1 - h01 * q0 - h11 * q1
    n1 = jnp.sqrt(inner(t1, t1) + epsilon)
    l00 = jnp.sqrt(h00 * h00 + n0 * n0)
    l10 = (h00 * h01 + n0 * h11) / l00
    l11 = jnp.sqrt(h01 * h01 + h11 * h11 + n1 * n1 - l10 * l10)
    z0 = beta * h00 / l00
    z1 = (beta * h01 - l10 * z0) / l11
    y1 = z1 / l11
    y0 = (z0 - l10 * y1) / l00
    c1 = y1 / (beta * n0)
    c0 = y0 / beta - h00 * c1
    planes, rows, depth = b_ref.shape
    for i in range(planes):
        b, image = b_ref[i], image_ref[i]
        solution_ref[i] = c0 * b + c1 * image
        residual_ref[i] = b - c0 * image - c1 * twice_ref[i]
    corners = by_turn(corner_first_ref[...], corner_second_ref[...], "gy")
    for side, (j, here, corner) in enumerate(zip((0, rows - 1), has_beside("gy"), corners)):
        for end, i in enumerate((0, planes - 1)):
            b, cond = corner[end : end + 1], corner[2 + end : 3 + end]
            cond = jnp.where(here, cond, 0.0)
            at = 6 * (2 * side + end)
            x_link, x_b, x_cond, y_link, y_b, y_cond = (
                ends_ref[at + k : at + k + 1] for k in range(6)
            )
            lacked = x_link * link(x_cond, cond) * (x_b - b)
            lacked = lacked + y_link * link(y_cond, cond) * (y_b - b)
            residual_ref[i, j : j + 1] = residual_ref[i, j : j + 1] + c1 * lacked


def call(kernel, shapes, *operands, scratch=(), inputs=pltpu.VMEM, flops=0):
    return pl.pallas_call(
        kernel,
        out_shape=[jax.ShapeDtypeStruct(shape, jnp.float32) for shape in shapes],
        in_specs=[pl.BlockSpec(memory_space=inputs)] * len(operands),
        out_specs=[pl.BlockSpec(memory_space=pltpu.VMEM)] * len(shapes),
        scratch_shapes=scratch,
        compiler_params=pltpu.CompilerParams(vmem_limit_bytes=48 * 1024 * 1024),
        cost_estimate=pl.CostEstimate(flops=flops, bytes_accessed=0, transcendentals=0),
    )(*operands)


def swap(first, second, axis):
    across = "gy" if axis == "gx" else "gx"
    count, lines = lax.axis_size(axis), lax.axis_size(across)

    def number(place, line):
        at = (place, line) if axis == "gx" else (line, place)
        return at[0] * lax.axis_size("gy") + at[1]

    turns = ([], [])
    for line in range(lines):
        for i in range(count):
            turns[0].append((number(i, line), number(i ^ 1, line)))
            beyond = i + 1 if i % 2 else i - 1
            if 0 <= beyond < count:
                turns[1].append((number(i, line), number(beyond, line)))
            else:
                turns[1].append((number(i, line), number(i, line ^ 1)))
    return [lax.ppermute(x, ("gx", "gy"), turn) for x, turn in zip((first, second), turns)]


def everyones(sketch):
    count = lax.axis_size("gx") * lax.axis_size("gy")
    copies = jnp.broadcast_to(sketch[None], (count,) + sketch.shape)
    return lax.all_to_all(copies, ("gx", "gy"), 0, 0)


def body(b, warmth, phase, slots, draw):
    planes, rows, depth = b.shape
    block, wide, table = b.shape, (planes + 2, rows, depth), (8, SKETCH)
    face, line, corner = (3 * rows + 4, depth), (3 * planes + 4, depth), (4, depth)
    cells = pltpu.VMEM((depth // LANES, (planes * rows + 8) * 8, LANES), jnp.float32)
    work = b.size * SKETCH * 6
    b, cond, cap, inner, draw, slots, x_first, x_second, y_first, y_second = call(
        first_kernel,
        [block] * 6 + [face, face, line, line],
        *(
            pltpu.with_memory_space_constraint(x, pltpu.HBM)
            for x in (b, warmth, phase, draw, slots)
        ),
        scratch=[
            pltpu.VMEM(block, warmth.dtype),
            pltpu.VMEM(block, phase.dtype),
            pltpu.VMEM(block, slots.dtype),
            pltpu.SemaphoreType.DMA((5,)),
        ],
        inputs=pltpu.HBM,
    )
    got_x = swap(x_first, x_second, "gx")
    got_y = swap(y_first, y_second, "gy")
    image_wide, beside, inside = call(
        inside_kernel,
        [wide, (4, rows, depth), table],
        b, cond, cap, inner, draw, slots, *got_x,
        scratch=[cells],
        flops=work,
    )
    image, twice, sketch, first, second, ends = call(
        third_kernel,
        [block, block, (FIELDS + 1, SKETCH), corner, corner, (24, depth)],
        b, cond, cap, draw, slots, image_wide, beside, *got_x, *got_y, inside,
        scratch=[cells, pltpu.VMEM((3, 8, depth), jnp.float32)],
        flops=work,
    )
    got_corners = swap(first, second, "gy")
    sketches = everyones(sketch)
    return tuple(
        call(last_kernel, [block, block], sketches, b, image, twice, ends, *got_corners)
    )


def solution(mesh):
    spec = P(("parts", "gx"), "gy", None)
    return jax.shard_map(
        body, mesh=mesh, in_specs=(spec,) * 5, out_specs=(spec,) * 2, check_vma=False
    )
```

time: 26.9 us -> 25 us (0.929)
  blocking collectives: 12.3 us -> 0 us
  starting transfers between devices: 7.04 us -> 12 us
  waiting for transfers between devices: 2.1 us -> 6.75 us
  local copies, waits for them, and re-layouts: 0.03 us -> 0.64 us
    all_to_all x1 -> x0, blocking collectives: 12.3 us -> none  [everyones(): return lax.all_to_all(copies, ('gx', 'gy'), 0, 0)]
    all_to_all x0 -> x1, starting transfers between devices: none -> 5.56 us  [everyones(): return lax.all_to_all(copies, ('gx', 'gy'), 0, 0)]
    all_to_all x0 -> x1, waiting for transfers between devices: none -> 2.56 us  [everyones(): return lax.all_to_all(copies, ('gx', 'gy'), 0, 0)]
    ppermute x6, waiting for transfers between devices: 2.1 us -> 4.19 us  [swap(): lax.ppermute(x, ('gx', 'gy'), turn)]
    broadcast_in_dim x1, local copies, waits for them, and re-layouts: 0.02 us -> 0.64 us  [everyones(): copies = jnp.broadcast_to(sketch[None], (count,) + sketch.shape)]
    ppermute x6, starting transfers between devices: 7.04 us -> 6.45 us  [swap(): lax.ppermute(x, ('gx', 'gy'), turn)]
    pallas_call x5 -> x4, Pallas kernels: 4.61 us -> 4.76 us  [call(): pl.pallas_call(kernel, out_shape=[jax.ShapeDtypeStruct(shape, jnp.float32...]
  transfers between devices with their start and end apart: 6 -> 7, of which waited for: 2 -> 4; matrix products, arithmetic and copies ran while one was open for 0% -> 0% of each run, Pallas kernels for 3% -> 3%
where the time goes in v1:
time: 25 us; the launch traced here: 24.8 us
  starting transfers between devices  12 us (48%)
  waiting for transfers between devices  6.75 us (27%)
  Pallas kernels  4.76 us (19%)
  between operations  0.66 us (3%)
  local copies, waits for them, and re-layouts  0.64 us (3%)
    ppermute x6, starting transfers between devices, swap(): lax.ppermute(x, ('gx', 'gy'), turn)  6.45 us
    all_to_all x1, starting transfers between devices, everyones(): return lax.all_to_all(copies, ('gx', 'gy'), 0, 0)  5.56 us
    pallas_call x4, Pallas kernels, call(): pl.pallas_call(kernel, out_shape=[jax.ShapeDtypeStruct(shape, jnp.float32...  4.76 us
    ppermute x6, waiting for transfers between devices, swap(): lax.ppermute(x, ('gx', 'gy'), turn)  4.19 us
    all_to_all x1, waiting for transfers between devices, everyones(): return lax.all_to_all(copies, ('gx', 'gy'), 0, 0)  2.56 us
    broadcast_in_dim x1, local copies, waits for them, and re-layouts, everyones(): copies = jnp.broadcast_to(sketch[None], (count,) + sketch.shape)  0.64 us
  transfers between devices with their start and end apart: 7, of which 4 were waited for; matrix products, arithmetic and copies ran while one was open for 0% of the time, Pallas kernels for 3%

profile of v1, /device:TPU:0, one launch (start us, length us, event | category | flops | bytes accessed | tf_op | source)
XLA Modules:
  0.0 24.8 jit_solution(7089106721445993971)
XLA Ops:
  0.6 1.5 %shard_map.68 = (f32[4,8,1024]{2,1,0:T(8,128)S(1)}, f32[4,8,1024]{2,1,0:T(8,128)S(1)}, f32[4,8,1024]{2,1,0:T(8,128)S(1)}, f32[4,8,1024]{2,1,0:T(8,128)S(1)}, f32...) custom-call(f32[4,8,1024]{2,1,0:T(8,128)} %b_hbm.1, ...), custom_call_target="tpu_custom_call" | custom-call | tf_op jit(solution)/shard_map/pallas_call | solution.py:341
  2.1 0.5 %collective-permute-start = (f32[28,1024]{1,0:T(8,128)S(1)}, f32[28,1024]{1,0:T(8,128)S(1)}, u32[]{:S(2)}, u32[]{:S(2)}) collective-permute-start(f32[28,1024]{1,0:T(8,128)S(1)} %get-tuple-element.27), channel_id=1, source_target_pairs={{0,4},{4,0},{8,12},{12,8},{1,5},{5,1},{9,13},{13,9},{2,6},{6,2},{1... | collective-permute-start | bytes 344072 | tf_op jit(solution)/shard_map/ppermute | solution.py:369
  2.6 2.6 %collective-permute-start.1 = (f32[28,1024]{1,0:T(8,128)S(1)}, f32[28,1024]{1,0:T(8,128)S(1)}, u32[]{:S(2)}, u32[]{:S(2)}) collective-permute-start(f32[28,1024]{1,0:T(8,128)S(1)} %get-tuple-element.28), channel_id=1, source_target_pairs={{0,1},{4,8},{8,4},{12,13},{1,0},{5,9},{9,5},{13,12},{2,3},{6,10},{... | collective-permute-start | bytes 344072 | tf_op jit(solution)/shard_map/ppermute | solution.py:369
  5.3 0.1 collective-permute-start.2
  5.3 1.3 %collective-permute-start.3 = (f32[16,1024]{1,0:T(8,128)S(1)}, f32[16,1024]{1,0:T(8,128)S(1)}, u32[]{:S(2)}, u32[]{:S(2)}) collective-permute-start(f32[16,1024]{1,0:T(8,128)S(1)} %get-tuple-element.32), channel_id=1, source_target_pairs={{0,4},{1,2},{2,1},{3,7},{4,0},{5,6},{6,5},{7,3},{8,12},{9,10},{10,... | collective-permute-start | bytes 196616 | tf_op jit(solution)/shard_map/ppermute | solution.py:369
  6.6 0.0 collective-permute-done.got_first_ref.x_first_ref
  6.6 1.9 %collective-permute-done.1.got_second_ref.x_second_ref = f32[28,1024]{1,0:T(8,128)S(1)} collective-permute-done((f32[28,1024]{1,0:T(8,128)S(1)}, f32[28,1024]{1,0:T(8,128)S(1)}, u32[]{:S(2)}, u32[]{:S(2)}) %collective-permute-start.1) | collective-permute-done | bytes 114720 | tf_op jit(solution)/shard_map/ppermute | solution.py:369
  8.5 0.8 %shard_map.69 = (f32[6,8,1024]{2,1,0:T(8,128)S(1)}, f32[4,8,1024]{2,1,0:T(8,128)S(1)}, f32[8,128]{1,0:T(8,128)S(1)}) custom-call(f32[4,8,1024]{2,1,0:T(8,128)S(1)} %get-tuple-element.21.b_ref, f32[4,8,1024]{2,1,0:T(8,128)S(1)} %get-tuple-element.22.cond_ref, f32[4,8,1024]{2,1,0:T(8,128)S(1)} %get-tuple-element.23.cap_ref, ...), custom_call_target="tpu_custom_call" | custom-call | flops 25165824 | tf_op jit(solution)/shard_map/pallas_call | solution.py:341
  9.3 0.3 %collective-permute-done.2.y_first_ref = f32[16,1024]{1,0:T(8,128)S(1)} collective-permute-done((f32[16,1024]{1,0:T(8,128)S(1)}, f32[16,1024]{1,0:T(8,128)S(1)}, u32[]{:S(2)}, u32[]{:S(2)}) %collective-permute-start.2) | collective-permute-done | bytes 65568 | tf_op jit(solution)/shard_map/ppermute | solution.py:369
  9.6 0.0 collective-permute-done.3.y_second_ref
  9.6 1.2 %shard_map.70 = (f32[4,8,1024]{2,1,0:T(8,128)S(1)}, f32[4,8,1024]{2,1,0:T(8,128)S(1)}, f32[4,128]{1,0:T(4,128)S(1)}, f32[4,1024]{1,0:T(4,128)S(1)}, f32[4,1024]{1,0:T(4,128)S(1)}, /*index=5*/f32[24,1024]{1,0:T(8,128)S(1)}) custom-call(f32[4,8,1024]{2,1,0:T(8,128)S(1)} %get-tuple-element.21.b_ref, f32[4,8,1024]{2,1,0:T(8,128)S(1)} %get-tuple-element.22.cond_ref, ...), custom_call_target="tpu_custom_call" | custom-call | flops 25165824 | tf_op jit(solution)/shard_map/pallas_call | solution.py:341
  10.9 0.6 %broadcast_in_dim.2 = f32[16,4,128]{2,1,0:T(4,128)} broadcast(f32[4,128]{1,0:T(4,128)S(1)} %get-tuple-element.34), dimensions={1,2} | broadcast | bytes 34816 | tf_op jit(solution)/shard_map/broadcast_in_dim | solution.py:374
  11.5 5.6 %all-to-all-start = ((f32[16,4,128]{2,1,0:T(4,128)}), f32[16,4,128]{2,1,0:T(4,128)S(1)}, u32[]{:S(2)}, u32[]{:S(2)}) async-start(f32[16,4,128]{2,1,0:T(4,128)} %broadcast_in_dim.2), calls=%async_computation | async-start | bytes 65536 | tf_op jit(solution)/shard_map/all_to_all | solution.py:375
  17.1 1.9 %collective-permute-start.4 = (f32[4,1024]{1,0:T(4,128)S(1)}, f32[4,1024]{1,0:T(4,128)S(1)}, u32[]{:S(2)}, u32[]{:S(2)}) collective-permute-start(f32[4,1024]{1,0:T(4,128)S(1)} %get-tuple-element.38), channel_id=1, source_target_pairs={{0,1},{1,0},{2,3},{3,2},{4,5},{5,4},{6,7},{7,6},{8,9},{9,8},{10,11... | collective-permute-start | bytes 49160 | tf_op jit(solution)/shard_map/ppermute | solution.py:369
  19.0 0.0 collective-permute-start.5
  19.0 2.0 %collective-permute-done.4.corner_first_ref = f32[4,1024]{1,0:T(4,128)S(1)} collective-permute-done((f32[4,1024]{1,0:T(4,128)S(1)}, f32[4,1024]{1,0:T(4,128)S(1)}, u32[]{:S(2)}, u32[]{:S(2)}) %collective-permute-start.4) | collective-permute-done | bytes 16416 | tf_op jit(solution)/shard_map/ppermute | solution.py:369
  21.0 0.0 collective-permute-done.5.corner_second_ref
  21.0 2.6 %all-to-all-done.sketch_ref = f32[16,4,128]{2,1,0:T(4,128)S(1)} async-done(((f32[16,4,128]{2,1,0:T(4,128)}), f32[16,4,128]{2,1,0:T(4,128)S(1)}, u32[]{:S(2)}, u32[]{:S(2)}) %all-to-all-start) | async-done | bytes 32800 | tf_op jit(solution)/shard_map/all_to_all | solution.py:375
  23.6 1.2 %shard_map.71 = (f32[4,8,1024]{2,1,0:T(8,128)}, f32[4,8,1024]{2,1,0:T(8,128)}) custom-call(f32[16,4,128]{2,1,0:T(4,128)S(1)} %all-to-all-done.sketch_ref, f32[4,8,1024]{2,1,0:T(8,128)S(1)} %get-tuple-element.21.b_ref, f32[4,8,1024]{2,1,0:T(8,128)S(1)} %get-tuple-element.35.image_ref, f32[4,8,1024]{2,1,0:T(8,128)S(1)} %get-tuple-element.36.twice_ref, ...), custom_call_target="tpu_custom_call" | custom-call | tf_op jit(solution)/shard_map/pallas_call | solution.py:341
Async XLA Ops:
  2.1 4.5 %collective-permute-start = (f32[28,1024]{1,0:T(8,128)S(1)}, f32[28,1024]{1,0:T(8,128)S(1)}, u32[]{:S(2)}, u32[]{:S(2)}) collective-permute-start(f32[28,1024]{1,0:T(8,128)S(1)} %get-tuple-element.27), channel_id=1, source_target_pairs={{0,4},{4,0},{8,12},{12,8},{1,5},{5,1},{9,13},{13,9},{2,6},{6,2},{1... | collective-permute-start | bytes 344072 | tf_op jit(solution)/shard_map/ppermute | solution.py:369
  2.6 5.9 %collective-permute-start.1 = (f32[28,1024]{1,0:T(8,128)S(1)}, f32[28,1024]{1,0:T(8,128)S(1)}, u32[]{:S(2)}, u32[]{:S(2)}) collective-permute-start(f32[28,1024]{1,0:T(8,128)S(1)} %get-tuple-element.28), channel_id=1, source_target_pairs={{0,1},{4,8},{8,4},{12,13},{1,0},{5,9},{9,5},{13,12},{2,3},{6,10},{... | collective-permute-start | bytes 344072 | tf_op jit(solution)/shard_map/ppermute | solution.py:369
  5.3 4.4 %collective-permute-start.2 = (f32[16,1024]{1,0:T(8,128)S(1)}, f32[16,1024]{1,0:T(8,128)S(1)}, u32[]{:S(2)}, u32[]{:S(2)}) collective-permute-start(f32[16,1024]{1,0:T(8,128)S(1)} %get-tuple-element.31), channel_id=1, source_target_pairs={{0,1},{1,0},{2,3},{3,2},{4,5},{5,4},{6,7},{7,6},{8,9},{9,8},{10,11... | collective-permute-start | bytes 196616 | tf_op jit(solution)/shard_map/ppermute | solution.py:369
  5.3 4.3 %collective-permute-start.3 = (f32[16,1024]{1,0:T(8,128)S(1)}, f32[16,1024]{1,0:T(8,128)S(1)}, u32[]{:S(2)}, u32[]{:S(2)}) collective-permute-start(f32[16,1024]{1,0:T(8,128)S(1)} %get-tuple-element.32), channel_id=1, source_target_pairs={{0,4},{1,2},{2,1},{3,7},{4,0},{5,6},{6,5},{7,3},{8,12},{9,10},{10,... | collective-permute-start | bytes 196616 | tf_op jit(solution)/shard_map/ppermute | solution.py:369
  11.5 12.1 %all-to-all-start = ((f32[16,4,128]{2,1,0:T(4,128)}), f32[16,4,128]{2,1,0:T(4,128)S(1)}, u32[]{:S(2)}, u32[]{:S(2)}) async-start(f32[16,4,128]{2,1,0:T(4,128)} %broadcast_in_dim.2), calls=%async_computation | async-start | bytes 65536 | tf_op jit(solution)/shard_map/all_to_all | solution.py:375
  17.1 3.9 %collective-permute-start.4 = (f32[4,1024]{1,0:T(4,128)S(1)}, f32[4,1024]{1,0:T(4,128)S(1)}, u32[]{:S(2)}, u32[]{:S(2)}) collective-permute-start(f32[4,1024]{1,0:T(4,128)S(1)} %get-tuple-element.38), channel_id=1, source_target_pairs={{0,1},{1,0},{2,3},{3,2},{4,5},{5,4},{6,7},{7,6},{8,9},{9,8},{10,11... | collective-permute-start | bytes 49160 | tf_op jit(solution)/shard_map/ppermute | solution.py:369
  19.0 2.0 %collective-permute-start.5 = (f32[4,1024]{1,0:T(4,128)S(1)}, f32[4,1024]{1,0:T(4,128)S(1)}, u32[]{:S(2)}, u32[]{:S(2)}) collective-permute-start(f32[4,1024]{1,0:T(4,128)S(1)} %get-tuple-element.39), channel_id=1, source_target_pairs={{0,4},{1,2},{2,1},{3,7},{4,0},{5,6},{6,5},{7,3},{8,12},{9,10},{10,... | collective-permute-start | bytes 49160 | tf_op jit(solution)/shard_map/ppermute | solution.py:369
